TPU v7x, 32 devices: a whole 2x2x4 slice. The times are simulated.
32 devices in a mesh: groups: 2 (over x), blk: 16 (over z, y, core).
Axes of the slice: x: 2, y: 2, z: 4, core: 2. Of those that a mesh axis runs over, the one named last changes fastest.
Arguments:
- queries: bfloat16 [32768, 1024], P(('groups', 'blk')), parts along dimension 0, may hold values from -2.5 to 2.5
- passages: bfloat16 [128, 256, 1024], P('blk', 'groups'), parts along dimension 1, may hold values from -12 to 12
- block_list: int32 [256, 4], P(('groups', 'blk')), parts along dimension 0, may hold values from 0 to 127, as said below
- pair_count: int32 [256], P(('groups', 'blk')), parts along dimension 0, may hold values from 1 to 4, 256 in all
- positive: int32 [32768], P(('groups', 'blk')), parts along dimension 0, may hold values from 0 to 511
Outputs:
- row_loss: float32 [32768], P(('groups', 'blk')), parts along dimension 0
- query_grad: bfloat16 [32768, 1024], P(('groups', 'blk')), parts along dimension 0
- passage_grad: bfloat16 [128, 256, 1024], P('blk', 'groups'), parts along dimension 1
There are 2 independent parts, one for each index of `groups`. A program takes and returns all parts, laid end to end along the dimension named above; each array names one. Nothing has to cross between parts.
Inputs may be any that keep to these rules, and one draw needn't show every extreme that they name: `block_list`: each row names 4 different passage blocks; the 8 rows of one index of blk (aligned runs of 8 rows) name exactly 8 different passage blocks in all, each of them in the same number of rows. `pair_count`: the 128 entries of one group sum to 256, and some entry of each group equals 4; the sum holds for each group separately, not over all groups together.
All inputs are finite; a program needn't handle non-finite values.
Results may differ from a plain program's by a relative error of at most 0.0039.
Values may be sent and summed in bfloat16 or wider, within the bound.
A program may use at most 128 MiB of HBM per device.

v0:
```python
import jax
import jax.numpy as jnp
from jax import lax
from jax.sharding import PartitionSpec as P

D = 1024
BLK = 128
NB = 4
DISTINCT = 8


def send_back(partial_value):
    return lax.all_to_all(partial_value, "blk", split_axis=0, concat_axis=1, tiled=True)


def body(queries, passages, block_list, pair_count, positive):
    qblocks_here = block_list.shape[0]
    listed = block_list.reshape(-1)
    pair_total = listed.shape[0]
    span_cols = NB * BLK
    ordered = jnp.sort(listed)
    fresh = jnp.concatenate([jnp.ones((1,), jnp.bool_), ordered[1:] != ordered[:-1]])
    rank_of = jnp.cumsum(fresh.astype(jnp.int32)) - 1
    wanted = jnp.full((DISTINCT,), -1, jnp.int32).at[rank_of].set(ordered)
    matches = listed[:, None] == wanted[None, :]
    slot_index = jnp.sum(
        matches.astype(jnp.int32) * jnp.arange(DISTINCT, dtype=jnp.int32)[None, :], axis=1
    )
    merge_table = matches.astype(jnp.float32)
    requests = lax.all_gather(jnp.maximum(wanted, 0), "blk", axis=0, tiled=True)
    served = passages[:, requests, :]
    fetched = lax.all_to_all(served, "blk", split_axis=1, concat_axis=0, tiled=True)
    candidates = fetched[:, slot_index, :].reshape(BLK, qblocks_here, NB, D)
    query_rows = queries.reshape(qblocks_here, BLK, D)
    scores = jnp.einsum(
        "grd,cgnd->grnc", query_rows, candidates, preferred_element_type=jnp.float32
    )
    scores = scores.reshape(qblocks_here, BLK, span_cols)
    columns = jnp.arange(span_cols, dtype=jnp.int32)
    live_limit = pair_count * BLK
    is_live = columns[None, None, :] < live_limit[:, None, None]
    target_slot = positive.reshape(qblocks_here, BLK) % live_limit[:, None]
    row_max = jnp.max(jnp.where(is_live, scores, -jnp.inf), axis=2, keepdims=True)
    weights = jnp.where(is_live, jnp.exp(scores - row_max), jnp.float32(0.0))
    row_sum = jnp.sum(weights, axis=2, keepdims=True)
    target = jnp.take_along_axis(scores, target_slot[:, :, None], axis=2)[:, :, 0]
    row_loss = row_max[:, :, 0] + jnp.log(row_sum[:, :, 0]) - target
    onehot = (columns[None, None, :] == target_slot[:, :, None]).astype(jnp.float32)
    grad_scores = (
        (weights / row_sum - onehot).astype(jnp.bfloat16).reshape(qblocks_here, BLK, NB, BLK)
    )
    contrib = jnp.einsum(
        "grnc,grd->cgnd", grad_scores, query_rows, preferred_element_type=jnp.float32
    )
    contrib = contrib.reshape(BLK, pair_total, D)
    partial_value = jnp.einsum("cpd,pk->ckd", contrib, merge_table, precision=lax.Precision.HIGHEST)
    query_grad = jnp.einsum(
        "grnc,cgnd->grd", grad_scores, candidates, preferred_element_type=jnp.float32
    ).astype(jnp.bfloat16)
    returned = send_back(partial_value)
    passage_grad = jnp.zeros(passages.shape, jnp.float32).at[:, requests, :].add(returned)
    return (row_loss.reshape(-1), query_grad.reshape(-1, D), passage_grad.astype(jnp.bfloat16))


def solution(mesh):
    return jax.shard_map(
        body,
        mesh=mesh,
        in_specs=(
            P(("groups", "blk"), None),
            P("blk", "groups", None),
            P(("groups", "blk"), None),
            P(("groups", "blk")),
            P(("groups", "blk")),
        ),
        out_specs=(P(("groups", "blk")), P(("groups", "blk"), None), P("blk", "groups", None)),
        check_vma=False,
    )
```

profile of v0, /device:TPU:15, one launch (start us, length us, event | category | flops | bytes accessed | tf_op | source)
XLA Modules:
  0.0 248.9 jit_solution(7454822869387522437)
XLA Ops:
  0.6 0.0 copy-start
  0.7 0.9 copy.39
  1.6 0.1 reshape.340
  1.6 1.6 sort.15
  3.2 0.1 compare_bitcast_fusion.2
  3.3 0.1 add_convert_fusion
  3.4 0.1 copy.40
  3.5 0.1 reduce-window.4
  3.6 0.1 fusion.9
  3.7 1.2 dynamic-slice
  5.6 0.7 scatter_custom_fusion
  6.3 0.1 maximum_dynamic-update-slice_fusion
  6.4 7.9 %all-reduce = s32[128]{0:T(128)S(1)} all-reduce(s32[128]{0:T(128)S(1)} %maximum_dynamic-update-slice_fusion), channel_id=1, replica_groups=mesh['groups'=2,'blk'=16] {'blk'}, use_global_device_ids=true, to_apply=%add | all-reduce | flops 128 | bytes 1024
  14.3 7.5 %gather_fusion = bf16[128,8,1024]{2,0,1:T(8,128)(2,1)} fusion(bf16[8,128,1024]{2,1,0:T(8,128)(2,1)} %param.6, s32[1024]{0:T(1024)S(1)} %pad_clamp_fusion.1), kind=kCustom, calls=%fused_computation | custom fusion | bytes 4194816 | tf_op jit(solution)/shard_map/gather | solution.py:31
  21.8 4.1 %copy.41 = bf16[8,128,1024]{2,0,1:T(8,128)(2,1)} copy(bf16[8,128,1024]{2,1,0:T(8,128)(2,1)} %bitcast.88) | data formatting | bytes 4194304 | tf_op jit(solution)/shard_map/gather | solution.py:31
  25.8 0.0 copy-start.3
  25.8 0.0 copy-start.2
  25.8 9.4 %all-to-all-start = ((bf16[8,128,1024]{2,0,1:T(8,128)(2,1)}), bf16[8,128,1024]{2,0,1:T(8,128)(2,1)}, u32[]{:S(2)}, u32[]{:S(2)}) async-start(bf16[8,128,1024]{2,0,1:T(8,128)(2,1)} %copy.41), calls=%async_computation | async-start | bytes 4194304 | tf_op jit(solution)/shard_map/all_to_all | solution.py:32
  35.3 0.1 fusion.11
  35.3 0.1 copy.44
  35.4 0.1 fusion.10
  35.6 0.0 copy-done.3
  35.6 0.1 broadcast_compare_fusion
  35.7 0.0 copy-done.2
  35.7 0.2 add_select_fusion
  35.9 46.9 %all-to-all-done = bf16[8,128,1024]{2,0,1:T(8,128)(2,1)} async-done(((bf16[8,128,1024]{2,0,1:T(8,128)(2,1)}), bf16[8,128,1024]{2,0,1:T(8,128)(2,1)}, u32[]{:S(2)}, u32[]{:S(2)}) %all-to-all-start) | async-done | bytes 2097184 | tf_op jit(solution)/shard_map/all_to_all | solution.py:32
  82.8 3.0 %copy.43 = bf16[16,8,8,1024]{3,2,1,0:T(8,128)(2,1)S(1)} copy(bf16[16,8,8,1024]{3,1,2,0:T(8,128)(2,1)} %bitcast.5) | data formatting | bytes 4194304 | tf_op jit(solution)/shard_map/all_to_all | solution.py:32
  85.8 2.5 copy.47
  88.3 6.5 %gather_fusion.1 = bf16[32,128,1024]{2,1,0:T(8,128)(2,1)} fusion(bf16[128,8,1024]{2,0,1:T(8,128)(2,1)} %copy.47, s32[1024]{0:T(1024)S(1)} %pad_clamp_fusion), kind=kCustom, calls=%fused_computation.1 | custom fusion | bytes 16777344 | tf_op jit(solution)/shard_map/gather | solution.py:33
  94.8 0.0 copy-done
  94.8 4.8 %fusion.5 = (f32[8,128]{1,0:T(8,128)S(1)}, f32[8,128,4,128]{3,1,2,0:T(8,128)S(1)}) fusion(pred[8,4,128]{2,1,0:T(4,128)(4,1)S(1)} %broadcast_compare_fusion, bf16[128,8,4,1024]{3,0,2,1:T(8,128)(2,1)} %bitcast.85, bf16[8,128,1024,1]{2,1,3,0:T(8,128)(2,1)S(1)} %bitcast.80), kind=kOutput, calls=%fused_computation.11 | convolution fusion | flops 1074789376 | bytes 12591104 | tf_op jit(solution)/shard_map/grd,cgnd->grnc/dot_general | solution.py:35
  99.6 0.0 copy-start.1
  99.6 0.7 fusion.8
  100.3 2.5 fusion.23
  102.8 0.0 copy-done.1
  102.8 13.3 %fusion.2 = f32[128,8,1024]{2,1,0:T(8,128)} fusion(f32[128,32,1024]{2,0,1:T(8,128)S(1)} %bitcast.82, s32[32]{0:T(128)S(1)} %reshape.340, s32[8]{0:T(128)S(1)} %scatter_custom_fusion), kind=kOutput, calls=%fused_computation.8 | convolution fusion | flops 402653440 | bytes 20971680 | tf_op jit(solution)/shard_map/cpd,pk->ckd/dot_general | solution.py:56
  116.1 4.9 %all-to-all-start.1 = ((f32[128,8,1024]{2,1,0:T(8,128)}), f32[128,8,1024]{2,1,0:T(8,128)}, u32[]{:S(2)}, u32[]{:S(2)}) async-start(f32[128,8,1024]{2,1,0:T(8,128)} %fusion.2), calls=%async_computation.1 | async-start | bytes 8388608 | tf_op jit(solution)/shard_map/all_to_all | solution.py:13
  121.0 0.2 compare_select_fusion.2
  121.3 14.8 %gather_fusion.2 = f32[1024]{0:T(1024)S(1)} fusion(f32[8,128,512]{1,2,0:T(8,128)} %bitcast.83, s32[1024]{0:T(1024)S(1)} %fusion.14), kind=kCustom, calls=%fused_computation.2 | custom fusion | bytes 20480 | tf_op jit(solution)/shard_map/jit(take_along_axis)/gather | solution.py:46
  136.0 0.1 rem.46
  136.1 0.7 bitcast_subtract_fusion.1
  136.8 7.3 %bitcast_convert_fusion = bf16[8,128,1024]{2,1,0:T(8,128)(2,1)} fusion(bf16[128,8,4,1024]{3,0,2,1:T(8,128)(2,1)} %bitcast.86, f32[8,128,4,128]{3,1,2,0:T(8,128)} %copy-done.1, s32[8,128]{1,0:T(8,128)S(1)} %add_select_fusion, s32[4,128]{1,0:T(4,128)S(1)} %multiply_add_fusion, f32[8,128]{1,0:T(8,128)S(1)} %fusion.8, f32[8,128]{1,0:T(8,128)S(1)} %get-tuple-element.20, ...), kind=kOutput, calls=%fused_computation.7 | convolution fusion | flops 1078460416 | bytes 12601344 | tf_op jit(solution)/shard_map/grnc,cgnd->grd/dot_general | solution.py:57
  144.2 69.3 %all-to-all-done.1 = f32[128,8,1024]{2,1,0:T(8,128)} async-done(((f32[128,8,1024]{2,1,0:T(8,128)}), f32[128,8,1024]{2,1,0:T(8,128)}, u32[]{:S(2)}, u32[]{:S(2)}) %all-to-all-start.1) | async-done | bytes 4194336 | tf_op jit(solution)/shard_map/all_to_all | solution.py:13
  213.5 7.7 %copy.50 = f32[8,16,8,1024]{3,0,2,1:T(8,128)} copy(f32[8,16,8,1024]{3,2,0,1:T(8,128)} %bitcast.33) | data formatting | bytes 8388608 | tf_op jit(solution)/shard_map/all_to_all | solution.py:13
  221.2 2.5 %broadcast_in_dim.50 = f32[8,128,1024]{2,0,1:T(8,128)} broadcast(f32[]{:T(128)} %constant.47.clone.1), dimensions={} | broadcast | bytes 4194308 | tf_op jit(solution)/shard_map/broadcast_in_dim | solution.py:61
  223.7 20.2 %scatter_fusion = f32[8,128,1024]{2,0,1:T(8,128)} fusion(f32[8,128,1024]{2,0,1:T(8,128)} %broadcast_in_dim.50, s32[128]{0:T(128)S(1)} %compare_select_fusion.6, f32[128,8,1024]{2,1,0:T(8,128)} %bitcast.84), kind=kCustom, calls=%fused_computation.4 | custom fusion | flops 1048576 | bytes 12583424 | tf_op jit(solution)/shard_map/scatter-add | solution.py:61
  243.9 2.5 %convert_element_type.30 = bf16[8,128,1024]{2,0,1:T(8,128)(2,1)S(1)} convert(f32[8,128,1024]{2,0,1:T(8,128)} %scatter_fusion) | non-fusion elementwise | flops 1048576 | bytes 6291456 | tf_op jit(solution)/shard_map/convert_element_type | solution.py:62
  246.4 2.5 copy.51
  (12 shorter events, 0.1 us)
Async XLA Ops:
  0.6 94.2 %copy-start = (bf16[1024,1024]{1,0:T(8,128)(2,1)S(1)}, bf16[1024,1024]{1,0:T(8,128)(2,1)}, u32[]{:S(2)}) copy-start(bf16[1024,1024]{1,0:T(8,128)(2,1)} %param.5) | copy-start | bytes 6291460
  25.8 9.7 %copy-start.3 = (s32[8]{0:T(128)S(1)}, s32[8]{0:T(128)}, u32[]{:S(2)}) copy-start(s32[8]{0:T(128)} %param.8) | copy-start | bytes 100
  25.8 9.8 %copy-start.2 = (s32[1024]{0:T(1024)S(1)}, s32[1024]{0:T(1024)}, u32[]{:S(2)}) copy-start(s32[1024]{0:T(1024)} %param.9) | copy-start | bytes 12292
  25.8 57.0 %all-to-all-start = ((bf16[8,128,1024]{2,0,1:T(8,128)(2,1)}), bf16[8,128,1024]{2,0,1:T(8,128)(2,1)}, u32[]{:S(2)}, u32[]{:S(2)}) async-start(bf16[8,128,1024]{2,0,1:T(8,128)(2,1)} %copy.41), calls=%async_computation | async-start | bytes 4194304 | tf_op jit(solution)/shard_map/all_to_all | solution.py:32
  99.6 3.2 %copy-start.1 = (f32[8,128,4,128]{3,1,2,0:T(8,128)}, f32[8,128,4,128]{3,1,2,0:T(8,128)S(1)}, u32[]{:S(2)}) copy-start(f32[8,128,4,128]{3,1,2,0:T(8,128)S(1)} %get-tuple-element.21) | copy-start | bytes 6291460
  116.1 97.4 %all-to-all-start.1 = ((f32[128,8,1024]{2,1,0:T(8,128)}), f32[128,8,1024]{2,1,0:T(8,128)}, u32[]{:S(2)}, u32[]{:S(2)}) async-start(f32[128,8,1024]{2,1,0:T(8,128)} %fusion.2), calls=%async_computation.1 | async-start | bytes 8388608 | tf_op jit(solution)/shard_map/all_to_all | solution.py:13
where the time goes:
time: 250 us; the launch traced here: 249 us
  waiting for transfers between devices  116 us (46%)
  local copies, waits for them, and re-layouts  54.2 us (22%)
  matrix products  27.9 us (11%)
  other arithmetic  26.9 us (11%)
  starting transfers between devices  14.3 us (6%)
  blocking collectives  7.89 us (3%)
    all_to_all x1, waiting for transfers between devices, send_back(): lax.all_to_all(partial_value, 'blk', split_axis=0, concat_axis=1, tiled=T...  69.3 us
    all_to_all x1, waiting for transfers between devices, body(): lax.all_to_all(served, 'blk', split_axis=1, concat_axis=0, tiled=True)  46.9 us
    scatter-add x1, other arithmetic, body(): jnp.zeros(passages.shape, jnp.float32).at[:, requests, :].add(returned)  20.2 us
    gather x1, local copies, waits for them, and re-layouts, body(): jnp.take_along_axis(scores, target_slot[:, :, None], axis=2)[:, :, 0]  14.8 us
    dot_general x1, matrix products, body(): jnp.einsum('cpd,pk->ckd', contrib, merge_table, precision=lax.Precision.H...  13.3 us
    gather x2, local copies, waits for them, and re-layouts, body(): served = passages[:, requests, :]  11.6 us
    all_to_all x1, starting transfers between devices, body(): lax.all_to_all(served, 'blk', split_axis=1, concat_axis=0, tiled=True)  9.42 us
    unnamed x1, blocking collectives  7.89 us
  transfers between devices with their start and end apart: 2, of which 2 were waited for; matrix products, arithmetic and copies ran while one was open for 10% of the time, Pallas kernels for 0%

commit v1 on v0

--- a/solution.py
+++ b/solution.py
@@ -7,6 +7,18 @@
 BLK = 128
 NB = 4
 DISTINCT = 8
+
+
+def rotated_exchange(value, axis, split, join):
+    ways, here = (lax.axis_size(axis), lax.axis_index(axis))
+    width = value.shape[split] // ways
+    turned = jnp.roll(value, -here * width, axis=split)
+    got = [lax.slice_in_dim(turned, 0, width, axis=split)]
+    for far in range(1, ways):
+        sent = lax.slice_in_dim(turned, far * width, (far + 1) * width, axis=split)
+        got.append(lax.ppermute(sent, axis, [(d, (d + far) % ways) for d in range(ways)]))
+    line = jnp.concatenate(got[::-1], axis=join)
+    return jnp.roll(line, (here + 1) * got[0].shape[join], axis=join)
 
 
 def send_back(partial_value):
@@ -29,7 +41,7 @@
     merge_table = matches.astype(jnp.float32)
     requests = lax.all_gather(jnp.maximum(wanted, 0), "blk", axis=0, tiled=True)
     served = passages[:, requests, :]
-    fetched = lax.all_to_all(served, "blk", split_axis=1, concat_axis=0, tiled=True)
+    fetched = rotated_exchange(served, "blk", 1, 0)
     candidates = fetched[:, slot_index, :].reshape(BLK, qblocks_here, NB, D)
     query_rows = queries.reshape(qblocks_here, BLK, D)
     scores = jnp.einsum(

time: 250 us -> 265 us (1.060)
  starting transfers between devices: 14.3 us -> 42.8 us
  waiting for transfers between devices: 116 us -> 95.1 us
  other arithmetic: 26.9 us -> 34.6 us
    all_to_all x1 -> x0, waiting for transfers between devices: 46.9 us -> none  [body(): lax.all_to_all(served, 'blk', split_axis=1, concat_axis=0, tiled=True)]
    ppermute x0 -> x15, starting transfers between devices: none -> 32.2 us  [rotated_exchange(): lax.ppermute(sent, axis, [(d, (d + far) % ways) for d in range(ways)])]
    ppermute x0 -> x15, waiting for transfers between devices: none -> 25.9 us  [rotated_exchange(): lax.ppermute(sent, axis, [(d, (d + far) % ways) for d in range(ways)])]
    all_to_all x1 -> x0, starting transfers between devices: 9.42 us -> none  [body(): lax.all_to_all(served, 'blk', split_axis=1, concat_axis=0, tiled=True)]
    all_to_all x1, starting transfers between devices: 4.91 us -> 10.6 us  [send_back(): lax.all_to_all(partial_value, 'blk', split_axis=0, concat_axis=1, tiled=T...]
    all_to_all x2 -> x0, local copies, waits for them, and re-layouts: 5.47 us -> none  [body(): lax.all_to_all(served, 'blk', split_axis=1, concat_axis=0, tiled=True)]
    gather x2 -> x1, local copies, waits for them, and re-layouts: 11.6 us -> 7.54 us  [body(): served = passages[:, requests, :]]
    unnamed x14 -> x65, local copies, waits for them, and re-layouts: 4.65 us -> 7.81 us
  transfers between devices with their start and end apart: 2 -> 16, of which waited for: 2 -> 10; matrix products, arithmetic and copies ran while one was open for 10% -> 11% of each run, Pallas kernels for 0% -> 0%
where the time goes in v1:
time: 265 us; the launch traced here: 264 us
  waiting for transfers between devices  95.1 us (36%)
  local copies, waits for them, and re-layouts  54.1 us (20%)
  starting transfers between devices  42.8 us (16%)
  other arithmetic  34.6 us (13%)
  matrix products  27.7 us (10%)
  blocking collectives  7.88 us (3%)
    all_to_all x1, waiting for transfers between devices, send_back(): lax.all_to_all(partial_value, 'blk', split_axis=0, concat_axis=1, tiled=T...  69.2 us
    ppermute x15, starting transfers between devices, rotated_exchange(): lax.ppermute(sent, axis, [(d, (d + far) % ways) for d in range(ways)])  32.2 us
    ppermute x15, waiting for transfers between devices, rotated_exchange(): lax.ppermute(sent, axis, [(d, (d + far) % ways) for d in range(ways)])  25.9 us
    scatter-add x1, other arithmetic, body(): jnp.zeros(passages.shape, jnp.float32).at[:, requests, :].add(returned)  20.4 us
    gather x1, local copies, waits for them, and re-layouts, body(): jnp.take_along_axis(scores, target_slot[:, :, None], axis=2)[:, :, 0]  14.8 us
    dot_general x1, matrix products, body(): jnp.einsum('cpd,pk->ckd', contrib, merge_table, precision=lax.Precision.H...  13.1 us
    all_to_all x1, starting transfers between devices, send_back(): lax.all_to_all(partial_value, 'blk', split_axis=0, concat_axis=1, tiled=T...  10.6 us
    unnamed x1, blocking collectives  7.88 us
  transfers between devices with their start and end apart: 16, of which 10 were waited for; matrix products, arithmetic and copies ran while one was open for 11% of the time, Pallas kernels for 0%

profile of v1, /device:TPU:15, one launch (start us, length us, event | category | flops | bytes accessed | tf_op | source)
XLA Modules:
  0.0 263.9 jit_solution(10511193232225717617)
XLA Ops:
  0.7 0.9 copy.19
  1.7 1.6 sort.15
  3.7 1.2 dynamic-slice
  6.3 1.2 broadcast_multiply_fusion
  7.5 7.9 %all-reduce = s32[128]{0:T(128)S(1)} all-reduce(s32[128]{0:T(128)S(1)} %get-tuple-element.31), channel_id=1, replica_groups=mesh['groups'=2,'blk'=16] {'blk'}, use_global_device_ids=true, to_apply=%add | all-reduce | flops 128 | bytes 1024
  16.0 7.5 %gather_fusion = bf16[128,8,1024]{2,0,1:T(8,128)(2,1)} fusion(bf16[8,128,1024]{2,1,0:T(8,128)(2,1)} %param.6, s32[1024]{0:T(1024)S(1)} %pad_clamp_fusion.1), kind=kCustom, calls=%fused_computation | custom fusion | bytes 4194816 | tf_op jit(solution)/shard_map/gather | solution.py:43
  23.5 2.7 %fusion.5 = bf16[8,128,1024]{2,1,0:T(8,128)(2,1)S(1)} fusion(s32[]{:T(128)S(6)} %select_n.134, bf16[8,128,1024]{2,1,0:T(8,128)(2,1)} %bitcast.83), kind=kLoop, calls=%fused_computation.11 | loop fusion | flops 4194304 | bytes 4194308 | tf_op jit(solution)/shard_map/jit(_roll_dynamic)/concatenate | solution.py:15
  26.3 1.3 copy-done.3
  27.6 1.0 fusion.25
  28.6 4.0 %collective-permute-start.14 = (bf16[8,8,1024]{2,1,0:T(8,128)(2,1)S(1)}, bf16[8,8,1024]{2,1,0:T(8,128)(2,1)S(1)}, u32[]{:S(2)}, u32[]{:S(2)}) collective-permute-start(bf16[8,8,1024]{2,1,0:T(8,128)(2,1)S(1)} %get-tuple-element.12), channel_id=1, source_target_pairs={{0,1},{1,2},{2,3},{3,4},{4,5},{5,6},{6,7},{7,8},{8,9},{9,10},{10,1... | collective-permute-start | bytes 393224 | tf_op jit(solution)/shard_map/ppermute | solution.py:19
  33.1 0.9 collective-permute-start.1
  34.0 1.3 collective-permute-start
  36.4 1.3 copy.21
  38.5 0.8 add_select_fusion
  39.3 0.8 fusion.11
  40.7 1.7 collective-permute-done
  42.5 3.1 %collective-permute-start.3 = (bf16[8,8,1024]{2,1,0:T(8,128)(2,1)}, bf16[8,8,1024]{2,1,0:T(8,128)(2,1)S(1)}, u32[]{:S(2)}, u32[]{:S(2)}) collective-permute-start(bf16[8,8,1024]{2,1,0:T(8,128)(2,1)} %get-tuple-element.23), channel_id=1, source_target_pairs={{0,12},{1,13},{2,14},{3,15},{4,0},{5,1},{6,2},{7,3},{8,4},{9,5},{1... | collective-permute-start | bytes 393224 | tf_op jit(solution)/shard_map/ppermute | solution.py:19
  45.6 3.2 %collective-permute-done.2 = bf16[8,8,1024]{2,1,0:T(8,128)(2,1)S(1)} collective-permute-done((bf16[8,8,1024]{2,1,0:T(8,128)(2,1)}, bf16[8,8,1024]{2,1,0:T(8,128)(2,1)S(1)}, u32[]{:S(2)}, u32[]{:S(2)}) %collective-permute-start.2) | collective-permute-done | bytes 131104 | tf_op jit(solution)/shard_map/ppermute | solution.py:19
  48.8 3.4 %collective-permute-start.4 = (bf16[8,8,1024]{2,1,0:T(8,128)(2,1)}, bf16[8,8,1024]{2,1,0:T(8,128)(2,1)S(1)}, u32[]{:S(2)}, u32[]{:S(2)}) collective-permute-start(bf16[8,8,1024]{2,1,0:T(8,128)(2,1)} %get-tuple-element.22), channel_id=1, source_target_pairs={{0,11},{1,12},{2,13},{3,14},{4,15},{5,0},{6,1},{7,2},{8,3},{9,4},{... | collective-permute-start | bytes 393224 | tf_op jit(solution)/shard_map/ppermute | solution.py:19
  52.3 2.5 collective-permute-start.5
  54.8 0.9 collective-permute-done.4
  55.7 1.7 collective-permute-start.6
  57.4 2.1 collective-permute-done.5
  59.5 8.4 %collective-permute-start.7 = (bf16[8,8,1024]{2,1,0:T(8,128)(2,1)}, bf16[8,8,1024]{2,1,0:T(8,128)(2,1)S(1)}, u32[]{:S(2)}, u32[]{:S(2)}) collective-permute-start(bf16[8,8,1024]{2,1,0:T(8,128)(2,1)} %get-tuple-element.19), channel_id=1, source_target_pairs={{0,8},{1,9},{2,10},{3,11},{4,12},{5,13},{6,14},{7,15},{8,0},{9,1},... | collective-permute-start | bytes 393224 | tf_op jit(solution)/shard_map/ppermute | solution.py:19
  68.0 3.1 %collective-permute-start.8 = (bf16[8,8,1024]{2,1,0:T(8,128)(2,1)}, bf16[8,8,1024]{2,1,0:T(8,128)(2,1)S(1)}, u32[]{:S(2)}, u32[]{:S(2)}) collective-permute-start(bf16[8,8,1024]{2,1,0:T(8,128)(2,1)} %get-tuple-element.18), channel_id=1, source_target_pairs={{0,7},{1,8},{2,9},{3,10},{4,11},{5,12},{6,13},{7,14},{8,15},{9,0},... | collective-permute-start | bytes 393224 | tf_op jit(solution)/shard_map/ppermute | solution.py:19
  71.1 5.9 %collective-permute-done.7 = bf16[8,8,1024]{2,1,0:T(8,128)(2,1)S(1)} collective-permute-done((bf16[8,8,1024]{2,1,0:T(8,128)(2,1)}, bf16[8,8,1024]{2,1,0:T(8,128)(2,1)S(1)}, u32[]{:S(2)}, u32[]{:S(2)}) %collective-permute-start.7) | collective-permute-done | bytes 131104 | tf_op jit(solution)/shard_map/ppermute | solution.py:19
  77.0 4.1 %collective-permute-done.8 = bf16[8,8,1024]{2,1,0:T(8,128)(2,1)S(1)} collective-permute-done((bf16[8,8,1024]{2,1,0:T(8,128)(2,1)}, bf16[8,8,1024]{2,1,0:T(8,128)(2,1)S(1)}, u32[]{:S(2)}, u32[]{:S(2)}) %collective-permute-start.8) | collective-permute-done | bytes 131104 | tf_op jit(solution)/shard_map/ppermute | solution.py:19
  81.1 1.6 collective-permute-start.10
  82.7 1.1 collective-permute-done.9
  83.8 1.7 collective-permute-start.11
  85.6 3.8 %collective-permute-done.10 = bf16[8,8,1024]{2,1,0:T(8,128)(2,1)S(1)} collective-permute-done((bf16[8,8,1024]{2,1,0:T(8,128)(2,1)S(1)}, bf16[8,8,1024]{2,1,0:T(8,128)(2,1)S(1)}, u32[]{:S(2)}, u32[]{:S(2)}) %collective-permute-start.10) | collective-permute-done | bytes 131104 | tf_op jit(solution)/shard_map/ppermute | solution.py:19
  89.4 2.9 %collective-permute-done.11 = bf16[8,8,1024]{2,1,0:T(8,128)(2,1)S(1)} collective-permute-done((bf16[8,8,1024]{2,1,0:T(8,128)(2,1)S(1)}, bf16[8,8,1024]{2,1,0:T(8,128)(2,1)S(1)}, u32[]{:S(2)}, u32[]{:S(2)}) %collective-permute-start.11) | collective-permute-done | bytes 131104 | tf_op jit(solution)/shard_map/ppermute | solution.py:19
  92.5 0.9 slice_dynamic-update-slice_fusion
  93.7 0.9 slice_dynamic-update-slice_fusion.1
  94.8 2.5 copy.24
  97.2 6.8 %gather_fusion.1 = bf16[32,128,1024]{2,1,0:T(8,128)(2,1)} fusion(bf16[128,8,1024]{2,0,1:T(8,128)(2,1)} %copy.24, s32[1024]{0:T(1024)} %pad_clamp_fusion), kind=kCustom, calls=%fused_computation.1 | custom fusion | bytes 16777344 | tf_op jit(solution)/shard_map/gather | solution.py:45
  104.1 4.8 %fusion.6 = (f32[8,128]{1,0:T(8,128)S(1)}, f32[8,128,4,128]{3,1,2,0:T(8,128)S(1)}) fusion(pred[8,4,128]{2,1,0:T(4,128)(4,1)S(1)} %broadcast_compare_fusion, bf16[128,8,4,1024]{3,0,2,1:T(8,128)(2,1)} %bitcast.81, bf16[8,128,1024,1]{2,1,3,0:T(8,128)(2,1)S(1)} %bitcast.76), kind=kOutput, calls=%fused_computation.14 | convolution fusion | flops 1074789376 | bytes 12591104 | tf_op jit(solution)/shard_map/grd,cgnd->grnc/dot_general | solution.py:47
  109.6 2.5 fusion.24
  112.1 13.1 %fusion.2 = f32[128,8,1024]{2,1,0:T(8,128)} fusion(f32[128,32,1024]{2,0,1:T(8,128)S(1)} %bitcast.78, s32[32]{0:T(128)S(1)} %copy-done.10, s32[8]{0:T(128)S(1)} %copy-done.12), kind=kOutput, calls=%fused_computation.10 | convolution fusion | flops 402653440 | bytes 20971680 | tf_op jit(solution)/shard_map/cpd,pk->ckd/dot_general | solution.py:68
  125.2 10.6 %all-to-all-start = ((f32[128,8,1024]{2,1,0:T(8,128)}), f32[128,8,1024]{2,1,0:T(8,128)}, u32[]{:S(2)}, u32[]{:S(2)}) async-start(f32[128,8,1024]{2,1,0:T(8,128)} %fusion.2), calls=%async_computation | async-start | bytes 8388608 | tf_op jit(solution)/shard_map/all_to_all | solution.py:25
  136.1 14.8 %gather_fusion.2 = f32[1024]{0:T(1024)S(1)} fusion(f32[8,128,512]{1,2,0:T(8,128)} %bitcast.79, s32[1024]{0:T(1024)S(1)} %fusion.15), kind=kCustom, calls=%fused_computation.2 | custom fusion | bytes 20480 | tf_op jit(solution)/shard_map/jit(take_along_axis)/gather | solution.py:58
  151.7 7.3 %bitcast_convert_fusion = bf16[8,128,1024]{2,1,0:T(8,128)(2,1)} fusion(bf16[128,8,4,1024]{3,0,2,1:T(8,128)(2,1)} %bitcast.82, f32[8,128,4,128]{3,1,2,0:T(8,128)} %copy-done.2, s32[8,128]{1,0:T(8,128)S(1)} %add_select_fusion, s32[4,128]{1,0:T(4,128)S(1)} %multiply_add_fusion, f32[8,128]{1,0:T(8,128)S(1)} %fusion.9, f32[8,128]{1,0:T(8,128)S(1)} %get-tuple-element.29, ...), kind=kOutput, calls=%fused_computation.9 | convolution fusion | flops 1078460416 | bytes 12601344 | tf_op jit(solution)/shard_map/grnc,cgnd->grd/dot_general | solution.py:69
  159.0 69.2 %all-to-all-done = f32[128,8,1024]{2,1,0:T(8,128)} async-done(((f32[128,8,1024]{2,1,0:T(8,128)}), f32[128,8,1024]{2,1,0:T(8,128)}, u32[]{:S(2)}, u32[]{:S(2)}) %all-to-all-start) | async-done | bytes 4194336 | tf_op jit(solution)/shard_map/all_to_all | solution.py:25
  228.3 7.7 %copy.27 = f32[8,16,8,1024]{3,0,2,1:T(8,128)} copy(f32[8,16,8,1024]{3,2,0,1:T(8,128)} %bitcast.29) | data formatting | bytes 8388608 | tf_op jit(solution)/shard_map/all_to_all | solution.py:25
  236.0 2.5 broadcast_in_dim.50
  238.5 20.4 %scatter_fusion = f32[8,128,1024]{2,0,1:T(8,128)} fusion(f32[8,128,1024]{2,0,1:T(8,128)} %broadcast_in_dim.50, s32[128]{0:T(128)S(1)} %copy-done.8, f32[128,8,1024]{2,1,0:T(8,128)} %bitcast.80), kind=kCustom, calls=%fused_computation.4 | custom fusion | flops 1048576 | bytes 12583424 | tf_op jit(solution)/shard_map/scatter-add | solution.py:73
  258.9 2.5 convert_element_type.30
  261.4 2.5 copy.28
  (92 shorter events, 7.1 us)
Async XLA Ops:
  0.6 103.5 %copy-start = (bf16[1024,1024]{1,0:T(8,128)(2,1)S(1)}, bf16[1024,1024]{1,0:T(8,128)(2,1)}, u32[]{:S(2)}) copy-start(bf16[1024,1024]{1,0:T(8,128)(2,1)} %param.5) | copy-start | bytes 6291460
  1.7 34.2 %copy-start.9 = (s32[32]{0:T(128)}, s32[32]{0:T(128)S(1)}, u32[]{:S(2)}) copy-start(s32[32]{0:T(128)S(1)} %reshape.340) | copy-start | bytes 388
  6.3 29.6 %copy-start.11 = (s32[8]{0:T(128)}, s32[8]{0:T(128)S(1)}, u32[]{:S(2)}) copy-start(s32[8]{0:T(128)S(1)} %scatter_custom_fusion) | copy-start | bytes 100
  15.4 0.6 copy-start.7
  23.5 11.8 %copy-start.13 = (s32[8]{0:T(128)S(1)}, s32[8]{0:T(128)}, u32[]{:S(2)}) copy-start(s32[8]{0:T(128)} %param.8) | copy-start | bytes 100
  23.5 14.9 %copy-start.4 = (s32[1024]{0:T(1024)S(1)}, s32[1024]{0:T(1024)}, u32[]{:S(2)}) copy-start(s32[1024]{0:T(1024)} %param.9) | copy-start | bytes 12292
  26.3 1.3 copy-start.3
  28.6 63.8 %collective-permute-start.14 = (bf16[8,8,1024]{2,1,0:T(8,128)(2,1)S(1)}, bf16[8,8,1024]{2,1,0:T(8,128)(2,1)S(1)}, u32[]{:S(2)}, u32[]{:S(2)}) collective-permute-start(bf16[8,8,1024]{2,1,0:T(8,128)(2,1)S(1)} %get-tuple-element.12), channel_id=1, source_target_pairs={{0,1},{1,2},{2,3},{3,4},{4,5},{5,6},{6,7},{7,8},{8,9},{9,10},{10,1... | collective-permute-start | bytes 393224 | tf_op jit(solution)/shard_map/ppermute | solution.py:19
  32.6 59.8 %collective-permute-start.13 = (bf16[8,8,1024]{2,1,0:T(8,128)(2,1)S(1)}, bf16[8,8,1024]{2,1,0:T(8,128)(2,1)S(1)}, u32[]{:S(2)}, u32[]{:S(2)}) collective-permute-start(bf16[8,8,1024]{2,1,0:T(8,128)(2,1)S(1)} %get-tuple-element.13), channel_id=1, source_target_pairs={{0,2},{1,3},{2,4},{3,5},{4,6},{5,7},{6,8},{7,9},{8,10},{9,11},{10,... | collective-permute-start | bytes 393224 | tf_op jit(solution)/shard_map/ppermute | solution.py:19
  33.1 59.2 %collective-permute-start.12 = (bf16[8,8,1024]{2,1,0:T(8,128)(2,1)S(1)}, bf16[8,8,1024]{2,1,0:T(8,128)(2,1)S(1)}, u32[]{:S(2)}, u32[]{:S(2)}) collective-permute-start(bf16[8,8,1024]{2,1,0:T(8,128)(2,1)S(1)} %get-tuple-element.14), channel_id=1, source_target_pairs={{0,3},{1,4},{2,5},{3,6},{4,7},{5,8},{6,9},{7,10},{8,11},{9,12},{10... | collective-permute-start | bytes 393224 | tf_op jit(solution)/shard_map/ppermute | solution.py:19
  33.1 9.3 %collective-permute-start.1 = (bf16[8,8,1024]{2,1,0:T(8,128)(2,1)}, bf16[8,8,1024]{2,1,0:T(8,128)(2,1)S(1)}, u32[]{:S(2)}, u32[]{:S(2)}) collective-permute-start(bf16[8,8,1024]{2,1,0:T(8,128)(2,1)} %get-tuple-element.25), channel_id=1, source_target_pairs={{0,14},{1,15},{2,0},{3,1},{4,2},{5,3},{6,4},{7,5},{8,6},{9,7},{10,... | collective-permute-start | bytes 393224 | tf_op jit(solution)/shard_map/ppermute | solution.py:19
  34.0 8.4 %collective-permute-start = (bf16[8,8,1024]{2,1,0:T(8,128)(2,1)}, bf16[8,8,1024]{2,1,0:T(8,128)(2,1)S(1)}, u32[]{:S(2)}, u32[]{:S(2)}) collective-permute-start(bf16[8,8,1024]{2,1,0:T(8,128)(2,1)} %get-tuple-element.26), channel_id=1, source_target_pairs={{0,15},{1,0},{2,1},{3,2},{4,3},{5,4},{6,5},{7,6},{8,7},{9,8},{10,9... | collective-permute-start | bytes 393224 | tf_op jit(solution)/shard_map/ppermute | solution.py:19
  42.4 6.4 %collective-permute-start.2 = (bf16[8,8,1024]{2,1,0:T(8,128)(2,1)}, bf16[8,8,1024]{2,1,0:T(8,128)(2,1)S(1)}, u32[]{:S(2)}, u32[]{:S(2)}) collective-permute-start(bf16[8,8,1024]{2,1,0:T(8,128)(2,1)} %get-tuple-element.24), channel_id=1, source_target_pairs={{0,13},{1,14},{2,15},{3,0},{4,1},{5,2},{6,3},{7,4},{8,5},{9,6},{10... | collective-permute-start | bytes 393224 | tf_op jit(solution)/shard_map/ppermute | solution.py:19
  42.5 9.8 %collective-permute-start.3 = (bf16[8,8,1024]{2,1,0:T(8,128)(2,1)}, bf16[8,8,1024]{2,1,0:T(8,128)(2,1)S(1)}, u32[]{:S(2)}, u32[]{:S(2)}) collective-permute-start(bf16[8,8,1024]{2,1,0:T(8,128)(2,1)} %get-tuple-element.23), channel_id=1, source_target_pairs={{0,12},{1,13},{2,14},{3,15},{4,0},{5,1},{6,2},{7,3},{8,4},{9,5},{1... | collective-permute-start | bytes 393224 | tf_op jit(solution)/shard_map/ppermute | solution.py:19
  48.8 6.9 %collective-permute-start.4 = (bf16[8,8,1024]{2,1,0:T(8,128)(2,1)}, bf16[8,8,1024]{2,1,0:T(8,128)(2,1)S(1)}, u32[]{:S(2)}, u32[]{:S(2)}) collective-permute-start(bf16[8,8,1024]{2,1,0:T(8,128)(2,1)} %get-tuple-element.22), channel_id=1, source_target_pairs={{0,11},{1,12},{2,13},{3,14},{4,15},{5,0},{6,1},{7,2},{8,3},{9,4},{... | collective-permute-start | bytes 393224 | tf_op jit(solution)/shard_map/ppermute | solution.py:19
  52.3 7.3 %collective-permute-start.5 = (bf16[8,8,1024]{2,1,0:T(8,128)(2,1)}, bf16[8,8,1024]{2,1,0:T(8,128)(2,1)S(1)}, u32[]{:S(2)}, u32[]{:S(2)}) collective-permute-start(bf16[8,8,1024]{2,1,0:T(8,128)(2,1)} %get-tuple-element.21), channel_id=1, source_target_pairs={{0,10},{1,11},{2,12},{3,13},{4,14},{5,15},{6,0},{7,1},{8,2},{9,3},... | collective-permute-start | bytes 393224 | tf_op jit(solution)/shard_map/ppermute | solution.py:19
  55.7 12.3 %collective-permute-start.6 = (bf16[8,8,1024]{2,1,0:T(8,128)(2,1)}, bf16[8,8,1024]{2,1,0:T(8,128)(2,1)S(1)}, u32[]{:S(2)}, u32[]{:S(2)}) collective-permute-start(bf16[8,8,1024]{2,1,0:T(8,128)(2,1)} %get-tuple-element.20), channel_id=1, source_target_pairs={{0,9},{1,10},{2,11},{3,12},{4,13},{5,14},{6,15},{7,0},{8,1},{9,2},... | collective-permute-start | bytes 393224 | tf_op jit(solution)/shard_map/ppermute | solution.py:19
  59.5 17.5 %collective-permute-start.7 = (bf16[8,8,1024]{2,1,0:T(8,128)(2,1)}, bf16[8,8,1024]{2,1,0:T(8,128)(2,1)S(1)}, u32[]{:S(2)}, u32[]{:S(2)}) collective-permute-start(bf16[8,8,1024]{2,1,0:T(8,128)(2,1)} %get-tuple-element.19), channel_id=1, source_target_pairs={{0,8},{1,9},{2,10},{3,11},{4,12},{5,13},{6,14},{7,15},{8,0},{9,1},... | collective-permute-start | bytes 393224 | tf_op jit(solution)/shard_map/ppermute | solution.py:19
  68.0 13.1 %collective-permute-start.8 = (bf16[8,8,1024]{2,1,0:T(8,128)(2,1)}, bf16[8,8,1024]{2,1,0:T(8,128)(2,1)S(1)}, u32[]{:S(2)}, u32[]{:S(2)}) collective-permute-start(bf16[8,8,1024]{2,1,0:T(8,128)(2,1)} %get-tuple-element.18), channel_id=1, source_target_pairs={{0,7},{1,8},{2,9},{3,10},{4,11},{5,12},{6,13},{7,14},{8,15},{9,0},... | collective-permute-start | bytes 393224 | tf_op jit(solution)/shard_map/ppermute | solution.py:19
  77.0 6.8 %collective-permute-start.9 = (bf16[8,8,1024]{2,1,0:T(8,128)(2,1)S(1)}, bf16[8,8,1024]{2,1,0:T(8,128)(2,1)S(1)}, u32[]{:S(2)}, u32[]{:S(2)}) collective-permute-start(bf16[8,8,1024]{2,1,0:T(8,128)(2,1)S(1)} %get-tuple-element.17), channel_id=1, source_target_pairs={{0,6},{1,7},{2,8},{3,9},{4,10},{5,11},{6,12},{7,13},{8,14},{9,15},... | collective-permute-start | bytes 393224 | tf_op jit(solution)/shard_map/ppermute | solution.py:19
  81.1 8.3 %collective-permute-start.10 = (bf16[8,8,1024]{2,1,0:T(8,128)(2,1)S(1)}, bf16[8,8,1024]{2,1,0:T(8,128)(2,1)S(1)}, u32[]{:S(2)}, u32[]{:S(2)}) collective-permute-start(bf16[8,8,1024]{2,1,0:T(8,128)(2,1)S(1)} %get-tuple-element.16), channel_id=1, source_target_pairs={{0,5},{1,6},{2,7},{3,8},{4,9},{5,10},{6,11},{7,12},{8,13},{9,14},{... | collective-permute-start | bytes 393224 | tf_op jit(solution)/shard_map/ppermute | solution.py:19
  83.8 8.5 %collective-permute-start.11 = (bf16[8,8,1024]{2,1,0:T(8,128)(2,1)S(1)}, bf16[8,8,1024]{2,1,0:T(8,128)(2,1)S(1)}, u32[]{:S(2)}, u32[]{:S(2)}) collective-permute-start(bf16[8,8,1024]{2,1,0:T(8,128)(2,1)S(1)} %get-tuple-element.15), channel_id=1, source_target_pairs={{0,4},{1,5},{2,6},{3,7},{4,8},{5,9},{6,10},{7,11},{8,12},{9,13},{1... | collective-permute-start | bytes 393224 | tf_op jit(solution)/shard_map/ppermute | solution.py:19
  108.9 3.2 %copy-start.2 = (f32[8,128,4,128]{3,1,2,0:T(8,128)}, f32[8,128,4,128]{3,1,2,0:T(8,128)S(1)}, u32[]{:S(2)}) copy-start(f32[8,128,4,128]{3,1,2,0:T(8,128)S(1)} %get-tuple-element.30) | copy-start | bytes 6291460
  109.6 2.5 copy-start.10
  109.6 2.5 copy-start.12
  125.2 10.6 %copy-start.5 = (s32[8]{0:T(128)S(1)}, s32[8]{0:T(128)}, u32[]{:S(2)}) copy-start(s32[8]{0:T(128)} %get-tuple-element.28) | copy-start | bytes 100
  125.2 10.6 %copy-start.6 = (pred[8]{0:T(512)(128)(4,1)S(1)}, pred[8]{0:T(512)(128)(4,1)}, u32[]{:S(2)}) copy-start(pred[8]{0:T(512)(128)(4,1)} %broadcast_compare_fusion.1) | copy-start | bytes 28
  125.2 103.0 %all-to-all-start = ((f32[128,8,1024]{2,1,0:T(8,128)}), f32[128,8,1024]{2,1,0:T(8,128)}, u32[]{:S(2)}, u32[]{:S(2)}) async-start(f32[128,8,1024]{2,1,0:T(8,128)} %fusion.2), calls=%async_computation | async-start | bytes 8388608 | tf_op jit(solution)/shard_map/all_to_all | solution.py:25
  236.0 2.5 copy-start.8
  238.5 25.4 %copy-start.1 = (bf16[1024,1024]{1,0:T(8,128)(2,1)S(1)}, bf16[1024,1024]{1,0:T(8,128)(2,1)}, u32[]{:S(2)}) copy-start(bf16[1024,1024]{1,0:T(8,128)(2,1)} %param.5) | copy-start | bytes 6291460
